TPU v7x, 32 devices: a whole 2x2x4 slice. The times are simulated.
32 devices in a mesh: group: 2 (over y), expert: 4 (over z), dp: 4 (over x, core).
Axes of the slice: x: 2, y: 2, z: 4, core: 2. Of those that a mesh axis runs over, the one named last changes fastest.
Arguments:
- tokens: bfloat16 [1024, 2048], P(('group', 'expert', 'dp')), parts along dimension 0, may hold values from -6 to 6
- out_grad: bfloat16 [1024, 2048], P(('group', 'expert', 'dp')), parts along dimension 0, may hold values from -0.59765625 to 0.59765625
- expert_ids: int32 [1024, 2], P(('group', 'expert', 'dp')), parts along dimension 0, may hold values from 0 to 3, all different within a row; in each aligned block of 32 rows (0 to 31, 32 to 63, ...) at most 24 rows name the same one
- combine: float32 [1024, 2], P(('group', 'expert', 'dp')), parts along dimension 0, may hold values from 0.1 to 0.6
- gate_weight: bfloat16 [4, 2048, 768], P('expert', 'dp'), may hold values from -0.125 to 0.125
- up_weight: bfloat16 [4, 2048, 768], P('expert', 'dp'), may hold values from -0.125 to 0.125
- down_t: bfloat16 [4, 2048, 768], P('expert', 'dp'), may hold values from -0.21875 to 0.21875
Outputs:
- mixed: bfloat16 [1024, 2048], P(('group', 'expert', 'dp')), parts along dimension 0
- down_grad: bfloat16 [8, 2048, 768], P(('group', 'expert'), 'dp'), parts along dimension 0
There are 2 independent parts, one for each index of `group`. A program takes and returns all parts, laid end to end along the dimension named above; an argument that names none is the same for every part. Nothing has to cross between parts.
Inputs may be any that keep to these rules, and one draw needn't show every extreme that they name: `expert_ids`: each row names 2 different experts. Among the 32 tokens of one device no expert is named by more than 24 of them, and in every draw some expert is named by exactly 24 tokens of some device.
All inputs are finite; a program needn't handle non-finite values.
Results may differ from a plain program's by a relative error of at most 0.012.
Values may be sent and summed in bfloat16 or wider, within the bound.
A program may use at most 64 MiB of HBM per device.

v0:
```python
import jax
import jax.numpy as jnp
from jax import lax
from jax.sharding import PartitionSpec as P

CAP = 24


def per_device(tokens, out_grad, expert_ids, combine, gate_weight, up_weight, down_t):
    experts = lax.axis_size("expert")
    tok_count, top_count = expert_ids.shape
    model_width = tokens.shape[1]
    slot_total = experts * CAP
    flat_ids = expert_ids.reshape(-1)
    onehot = (flat_ids[:, None] == jnp.arange(experts, dtype=jnp.int32)[None, :]).astype(jnp.int32)
    earlier = jnp.sum((jnp.cumsum(onehot, 0) - onehot) * onehot, 1)
    target = flat_ids * CAP + earlier
    sources = jnp.arange(tok_count * top_count, dtype=jnp.int32) // top_count
    slot_token = jnp.full((slot_total,), tok_count, jnp.int32).at[target].set(sources)
    slot_weight = jnp.zeros((slot_total,), jnp.float32).at[target].set(combine.reshape(-1))
    padded_rows = jnp.concatenate([tokens, jnp.zeros((1, model_width), jnp.bfloat16)], 0)
    padded_grad = jnp.concatenate([out_grad, jnp.zeros((1, model_width), jnp.bfloat16)], 0)
    send_rows = padded_rows[slot_token].reshape(experts, CAP, model_width)
    send_grad = (slot_weight[:, None] * padded_grad[slot_token].astype(jnp.float32)).astype(
        jnp.bfloat16
    )
    send_grad = send_grad.reshape(experts, CAP, model_width)
    recv_rows = lax.all_to_all(send_rows, "expert", split_axis=0, concat_axis=0, tiled=True)
    expert_rows = recv_rows.reshape(slot_total, model_width)
    gate_shard = gate_weight[0]
    up_shard = up_weight[0]
    down_shard = down_t[0]

    def add_rows(shard_piece):
        return jnp.dot(expert_rows, shard_piece, preferred_element_type=jnp.float32)

    gate_sum = add_rows(lax.all_gather(gate_shard, "dp", axis=0, tiled=True))
    up_sum = add_rows(lax.all_gather(up_shard, "dp", axis=0, tiled=True))
    hidden = (jax.nn.silu(gate_sum) * up_sum).astype(jnp.bfloat16)
    product = lax.dot_general(
        hidden,
        lax.all_gather(down_shard, "dp", axis=0, tiled=True),
        (((1,), (1,)), ((), ())),
        preferred_element_type=jnp.float32,
    )
    expert_out = product.astype(jnp.bfloat16)
    returned = lax.all_to_all(
        expert_out.reshape(experts, CAP, model_width),
        "expert",
        split_axis=0,
        concat_axis=0,
        tiled=True,
    )
    returned = returned.reshape(slot_total, model_width)[target]
    mixed = jnp.sum(
        returned.reshape(tok_count, top_count, model_width).astype(jnp.float32)
        * combine[:, :, None],
        1,
    )
    mixed = mixed.astype(jnp.bfloat16)
    recv_grad = lax.all_to_all(send_grad, "expert", split_axis=0, concat_axis=0, tiled=True)
    grad_rows = recv_grad.reshape(slot_total, model_width)
    own_grad = lax.psum_scatter(
        lax.dot_general(
            grad_rows, hidden, (((0,), (0,)), ((), ())), preferred_element_type=jnp.float32
        ).astype(jnp.bfloat16),
        "dp",
        scatter_dimension=0,
        tiled=True,
    )
    down_grad = own_grad[None]
    return (mixed, down_grad)


def solution(mesh):
    in_specs = (
        P(("group", "expert", "dp"), None),
        P(("group", "expert", "dp"), None),
        P(("group", "expert", "dp"), None),
        P(("group", "expert", "dp"), None),
        P("expert", "dp", None),
        P("expert", "dp", None),
        P("expert", "dp", None),
    )
    out_specs = (P(("group", "expert", "dp"), None), P(("group", "expert"), "dp", None))
    return jax.shard_map(
        per_device, mesh=mesh, in_specs=in_specs, out_specs=out_specs, check_vma=False
    )
```

profile of v0, /device:TPU:0, one launch (start us, length us, event | category | flops | bytes accessed | tf_op | source)
XLA Modules:
  0.0 148.6 jit_solution(18128228273816271385)
XLA Ops:
  8.0 0.7 all-gather.9.cloned.1.call-update
  9.4 0.8 copy.14
  10.3 0.7 broadcast_multiply_fusion
  11.3 0.9 concatenate.6
  12.4 0.8 scatter_custom_fusion
  13.3 1.6 %gather_fusion = bf16[96,2048]{1,0:T(8,128)(2,1)} fusion(bf16[33,2048]{1,0:T(8,128)(2,1)S(1)} %concatenate.6, s32[1024]{0:T(1024)S(1)} %pad_clamp_fusion.1), kind=kCustom, calls=%fused_computation | custom fusion | bytes 786816 | tf_op jit(solution)/shard_map/gather | solution.py:23
  14.8 6.4 %all-to-all-start = ((bf16[4,24,2048]{2,1,0:T(8,128)(2,1)}), bf16[4,24,2048]{2,1,0:T(8,128)(2,1)S(1)}, u32[]{:S(2)}, u32[]{:S(2)}) async-start(bf16[4,24,2048]{2,1,0:T(8,128)(2,1)} %bitcast.2), calls=%async_computation | async-start | bytes 786432 | tf_op jit(solution)/shard_map/all_to_all | solution.py:28
  21.3 0.8 gather_fusion.2
  22.3 0.8 scatter_custom_fusion.1
  23.2 0.9 fusion.15
  24.1 8.9 %all-to-all-done = bf16[4,24,2048]{2,1,0:T(8,128)(2,1)S(1)} async-done(((bf16[4,24,2048]{2,1,0:T(8,128)(2,1)}), bf16[4,24,2048]{2,1,0:T(8,128)(2,1)S(1)}, u32[]{:S(2)}, u32[]{:S(2)}) %all-to-all-start) | async-done | bytes 393248 | tf_op jit(solution)/shard_map/all_to_all | solution.py:28
  33.0 3.5 %all-to-all-start.2 = ((bf16[4,24,2048]{2,1,0:T(8,128)(2,1)}), bf16[4,24,2048]{2,1,0:T(8,128)(2,1)S(1)}, u32[]{:S(2)}, u32[]{:S(2)}) async-start(bf16[4,24,2048]{2,1,0:T(8,128)(2,1)} %fusion.15), calls=%async_computation.2 | async-start | bytes 786432 | tf_op jit(solution)/shard_map/all_to_all | solution.py:61
  36.5 4.3 %all-gather.7.cloned.1.call-done = bf16[1,2048,768]{2,1,0:T(8,128)(2,1)} async-done(((bf16[1,512,768]{2,1,0:T(8,128)(2,1)}), bf16[1,2048,768]{2,1,0:T(8,128)(2,1)}) %all-gather.7.cloned.1.call-update) | async-done | bytes 3145744 | tf_op jit(solution)/shard_map/all_gather | solution.py:37
  40.8 2.5 %fusion.4 = f32[96,768]{1,0:T(8,128)S(1)} fusion(bf16[96,2048]{1,0:T(8,128)(2,1)S(1)} %bitcast.35, bf16[1,2048,768]{2,1,0:T(8,128)(2,1)} %all-gather.7.cloned.1.call-done), kind=kOutput, calls=%fused_computation.10 | convolution fusion | flops 301989888 | bytes 3833856 | tf_op jit(solution)/shard_map/dot_general | solution.py:35
  43.3 27.6 %all-gather.9.cloned.1.call-done = bf16[1,2048,768]{2,1,0:T(8,128)(2,1)} async-done(((bf16[1,512,768]{2,1,0:T(8,128)(2,1)}), bf16[1,2048,768]{2,1,0:T(8,128)(2,1)}) %all-gather.9.cloned.1.call-update) | async-done | bytes 3145744 | tf_op jit(solution)/shard_map/all_gather | solution.py:38
  70.9 2.5 %fusion.12 = bf16[96,768]{1,0:T(8,128)(2,1)S(1)} fusion(bf16[96,2048]{1,0:T(8,128)(2,1)S(1)} %bitcast.36, bf16[1,2048,768]{2,1,0:T(8,128)(2,1)} %all-gather.9.cloned.1.call-done, f32[96,768]{1,0:T(8,128)S(1)} %fusion.4), kind=kOutput, calls=%fused_computation.14 | convolution fusion | flops 302432256 | bytes 3981312 | tf_op jit(solution)/shard_map/dot_general | solution.py:35
  73.5 2.7 %convolution_convert_fusion = bf16[2048,768]{1,0:T(8,128)(2,1)} fusion(bf16[96,2048]{1,0:T(8,128)(2,1)S(1)} %bitcast.37, bf16[96,768]{1,0:T(8,128)(2,1)S(1)} %fusion.12), kind=kOutput, calls=%fused_computation.5 | convolution fusion | flops 303562752 | bytes 3686400 | tf_op jit(solution)/shard_map/dot_general | solution.py:64
  76.2 24.9 %all-gather.11.cloned.1.call-done = bf16[1,2048,768]{2,1,0:T(8,128)(2,1)} async-done(((bf16[1,512,768]{2,1,0:T(8,128)(2,1)}), bf16[1,2048,768]{2,1,0:T(8,128)(2,1)}) %all-gather.11.cloned.1.call-update) | async-done | bytes 3145744 | tf_op jit(solution)/shard_map/all_gather | solution.py:42
  101.1 3.7 %fusion.6 = bf16[96,2048]{1,0:T(8,128)(2,1)} fusion(bf16[96,768]{1,0:T(8,128)(2,1)S(1)} %fusion.12, bf16[1,2048,768]{2,1,0:T(8,128)(2,1)} %all-gather.11.cloned.1.call-done), kind=kOutput, calls=%fused_computation.12 | convolution fusion | flops 302186496 | bytes 3686400 | tf_op jit(solution)/shard_map/dot_general | solution.py:40
  104.8 4.6 %all-to-all-start.1 = ((bf16[4,24,2048]{2,1,0:T(8,128)(2,1)}), bf16[4,24,2048]{2,1,0:T(8,128)(2,1)S(1)}, u32[]{:S(2)}, u32[]{:S(2)}) async-start(bf16[4,24,2048]{2,1,0:T(8,128)(2,1)} %bitcast.7), calls=%async_computation.1 | async-start | bytes 786432 | tf_op jit(solution)/shard_map/all_to_all | solution.py:47
  109.4 12.1 %all-to-all-done.1 = bf16[4,24,2048]{2,1,0:T(8,128)(2,1)S(1)} async-done(((bf16[4,24,2048]{2,1,0:T(8,128)(2,1)}), bf16[4,24,2048]{2,1,0:T(8,128)(2,1)S(1)}, u32[]{:S(2)}, u32[]{:S(2)}) %all-to-all-start.1) | async-done | bytes 393248 | tf_op jit(solution)/shard_map/all_to_all | solution.py:47
  121.5 0.7 gather_fusion.1
  122.6 1.4 multiply_reduce_fusion
  124.0 18.1 %reduce-scatter.2.cloned.1.call-done = bf16[512,768]{1,0:T(8,128)(2,1)} async-done(((bf16[2048,768]{1,0:T(8,128)(2,1)}), bf16[512,768]{1,0:T(8,128)(2,1)}) %reduce-scatter.2.cloned.1.call-update) | async-done | bytes 786448 | tf_op jit(solution)/shard_map/reduce_scatter | solution.py:63
  (28 shorter events, 2.8 us)
Async XLA Ops:
  7.2 33.7 %all-gather.7.cloned.1.call-start = ((), (), s32[]{:S(2)}) async-start(), calls=%async_computation.5 | async-start | bytes 3932160 | tf_op jit(solution)/shard_map/all_gather | solution.py:37
  7.9 13.4 %copy-start = (bf16[32,2048]{1,0:T(8,128)(2,1)S(1)}, bf16[32,2048]{1,0:T(8,128)(2,1)}, u32[]{:S(2)}) copy-start(bf16[32,2048]{1,0:T(8,128)(2,1)} %param.8) | copy-start | bytes 393220
  7.9 63.0 %all-gather.9.cloned.1.call-start = ((), (), s32[]{:S(2)}) async-start(), calls=%async_computation.6 | async-start | bytes 3932160 | tf_op jit(solution)/shard_map/all_gather | solution.py:38
  8.7 92.4 %all-gather.11.cloned.1.call-start = ((), (), s32[]{:S(2)}) async-start(), calls=%async_computation.7 | async-start | bytes 3932160 | tf_op jit(solution)/shard_map/all_gather | solution.py:42
  14.8 7.3 %copy-start.1 = (f32[32,2]{0,1:T(2,128)S(1)}, f32[32,2]{0,1:T(2,128)}, u32[]{:S(2)}) copy-start(f32[32,2]{0,1:T(2,128)} %param.10) | copy-start | bytes 772
  14.8 18.1 %all-to-all-start = ((bf16[4,24,2048]{2,1,0:T(8,128)(2,1)}), bf16[4,24,2048]{2,1,0:T(8,128)(2,1)S(1)}, u32[]{:S(2)}, u32[]{:S(2)}) async-start(bf16[4,24,2048]{2,1,0:T(8,128)(2,1)} %bitcast.2), calls=%async_computation | async-start | bytes 786432 | tf_op jit(solution)/shard_map/all_to_all | solution.py:28
  33.0 40.5 %all-to-all-start.2 = ((bf16[4,24,2048]{2,1,0:T(8,128)(2,1)}), bf16[4,24,2048]{2,1,0:T(8,128)(2,1)S(1)}, u32[]{:S(2)}, u32[]{:S(2)}) async-start(bf16[4,24,2048]{2,1,0:T(8,128)(2,1)} %fusion.15), calls=%async_computation.2 | async-start | bytes 786432 | tf_op jit(solution)/shard_map/all_to_all | solution.py:61
  36.4 105.6 %reduce-scatter.2.cloned.1.call-start = ((), (), s32[]{:S(2)}) async-start(), calls=%async_computation.4 | async-start | bytes 3932160 | tf_op jit(solution)/shard_map/reduce_scatter | solution.py:63
  104.8 16.7 %all-to-all-start.1 = ((bf16[4,24,2048]{2,1,0:T(8,128)(2,1)}), bf16[4,24,2048]{2,1,0:T(8,128)(2,1)S(1)}, u32[]{:S(2)}, u32[]{:S(2)}) async-start(bf16[4,24,2048]{2,1,0:T(8,128)(2,1)} %bitcast.7), calls=%async_computation.1 | async-start | bytes 786432 | tf_op jit(solution)/shard_map/all_to_all | solution.py:47
Sparse Core Ops, SparseCore 0:
  9.6 31.2 all-gather.6
  42.4 28.5 all-gather.8
  72.5 28.5 all-gather.10
  104.0 37.9 reduce-scatter.1
where the time goes:
time: 149 us
  waiting for transfers between devices  97.9 us (66%)
  starting transfers between devices  14.7 us (10%)
  between operations  13.9 us (9%)
  matrix products  11.5 us (8%)
  local copies, waits for them, and re-layouts  7.33 us (5%)
  other arithmetic  3.33 us (2%)
    all_gather x1, waiting for transfers between devices, per_device(): up_sum = add_rows(lax.all_gather(up_shard, 'dp', axis=0, tiled=True))  27.6 us
    all_gather x1, waiting for transfers between devices, per_device(): lax.all_gather(down_shard, 'dp', axis=0, tiled=True)  24.9 us
    reduce_scatter x1, waiting for transfers between devices, per_device(): lax.psum_scatter(lax.dot_general(grad_rows, hidden, (((0,), (0,)), ((), (...  18.1 us
    all_to_all x1, waiting for transfers between devices, per_device(): lax.all_to_all(expert_out.reshape(experts, CAP, model_width), 'expert', s...  12.1 us
    all_to_all x1, waiting for transfers between devices, per_device(): lax.all_to_all(send_rows, 'expert', split_axis=0, concat_axis=0, tiled=True)  8.86 us
    all_to_all x1, starting transfers between devices, per_device(): lax.all_to_all(send_rows, 'expert', split_axis=0, concat_axis=0, tiled=True)  6.45 us
    dot_general x2, matrix products, add_rows(): return jnp.dot(expert_rows, shard_piece, preferred_element_type=jnp.float32)  5.07 us
    all_to_all x1, starting transfers between devices, per_device(): lax.all_to_all(expert_out.reshape(experts, CAP, model_width), 'expert', s...  4.6 us
  transfers between devices with their start and end apart: 7, of which 6 were waited for; matrix products, arithmetic and copies ran while one was open for 15% of the time, Pallas kernels for 0%

commit v1 on v0

--- a/solution.py
+++ b/solution.py
@@ -1,12 +1,355 @@
+import functools
+
 import jax
 import jax.numpy as jnp
 from jax import lax
+from jax.experimental import pallas as pl
+from jax.experimental.pallas import tpu as pltpu
 from jax.sharding import PartitionSpec as P
 
 CAP = 24
-
-
-def per_device(tokens, out_grad, expert_ids, combine, gate_weight, up_weight, down_t):
+MESH = pl.DeviceIdType.MESH
+F32 = jnp.float32
+BF16 = jnp.bfloat16
+
+
+def dot(a, b, dims=((1,), (0,))):
+    return lax.dot_general(a, b, (dims, ((), ())), preferred_element_type=F32)
+
+
+def kernel(
+    experts,
+    replicas,
+    tokens,
+    out_grad,
+    expert_ids,
+    combine,
+    gate_hbm,
+    up_hbm,
+    down_hbm,
+    mixed,
+    down_grad,
+    gate_w,
+    up_w,
+    down_w,
+    tok_send,
+    tok_recv,
+    grad_send,
+    grad_recv,
+    ret_send,
+    ret_recv,
+    mate_send,
+    mate_recv,
+    cross_send,
+    cross_recv,
+    own_sum,
+    hid,
+    load_sem,
+    tok_ssem,
+    tok_rsem,
+    grad_ssem,
+    grad_rsem,
+    ret_ssem,
+    ret_rsem,
+    mate_ssem,
+    mate_rsem,
+    cross_ssem,
+    cross_rsem,
+    hid_ssem,
+    hid_rsem,
+    fwd_ssem,
+    fwd_rsem,
+):
+    width = gate_hbm.shape[0]
+    half = width // 2
+    ff = gate_hbm.shape[1]
+    rows = experts * CAP
+    chips = replicas // 2
+    e = lax.axis_index("expert")
+    r = lax.axis_index("dp")
+    chip = r // 2
+    core = r % 2
+    me = r * experts + e
+    mate = {"dp": chip * 2 + 1 - core}
+
+    loads = [
+        pltpu.make_async_copy(src, dst, load_sem.at[i])
+        for i, (src, dst) in enumerate(((gate_hbm, gate_w), (up_hbm, up_w), (down_hbm, down_w)))
+    ]
+    for load in loads:
+        load.start()
+
+    peers = []
+    for dr in range(replicas):
+        for de in range(experts):
+            if dr or de:
+                pe, pr = lax.rem(e + de, experts), lax.rem(r + dr, replicas)
+                peers.append((pe, pr, pr * experts + pe))
+    barrier = pltpu.get_barrier_semaphore()
+    for pe, pr, _ in peers:
+        pl.semaphore_signal(barrier, inc=1, device_id={"expert": pe, "dp": pr}, device_id_type=MESH)
+
+    def exchange(src, dst, ssem, rsem):
+        copies = []
+        for pe, pr, n in peers:
+            copies.append(
+                (
+                    pltpu.make_async_remote_copy(
+                        src_ref=src.at[n],
+                        dst_ref=dst.at[me],
+                        send_sem=ssem.at[n],
+                        recv_sem=rsem.at[me],
+                        device_id={"expert": pe, "dp": pr},
+                        device_id_type=MESH,
+                    ),
+                    pltpu.make_async_remote_copy(
+                        src_ref=src.at[n],
+                        dst_ref=dst.at[n],
+                        send_sem=ssem.at[n],
+                        recv_sem=rsem.at[n],
+                        device_id={"expert": pe, "dp": pr},
+                        device_id_type=MESH,
+                    ),
+                )
+            )
+        return copies
+
+    def slab(block):
+        return jnp.concatenate([block[:, :half], block[:, half:]], 0).astype(BF16)
+
+    def fill(dst, value):
+        for pr in range(replicas):
+            for pe in range(experts):
+                dst[pr * experts + pe] = slab(
+                    value[pe * CAP : (pe + 1) * CAP, pr * width : (pr + 1) * width]
+                )
+
+    tok_count = tokens.shape[0]
+    top = expert_ids.shape[1]
+    column = lax.broadcasted_iota(jnp.int32, (tok_count, rows), 1)
+    owner = jnp.zeros((tok_count, rows), jnp.int32)
+    for j in range(1, experts):
+        owner = owner + (column >= j * CAP).astype(jnp.int32)
+    place = (column - owner * CAP).astype(F32)
+    picks = [(expert_ids[:, k : k + 1] == owner).astype(F32) for k in range(top)]
+    named = functools.reduce(jnp.add, picks)
+    earlier = (
+        lax.broadcasted_iota(jnp.int32, (tok_count, tok_count), 0)
+        > lax.broadcasted_iota(jnp.int32, (tok_count, tok_count), 1)
+    ).astype(F32)
+    slot = dot(earlier.astype(BF16), named.astype(BF16))
+    here = jnp.where(slot == place, 1.0, 0.0)
+    choice = jnp.concatenate([pick * here for pick in picks], 0).astype(BF16)
+    either = (named * here).astype(BF16)
+    fill(tok_send, dot(either, tokens[...], ((0,), (0,))))
+    pl.semaphore_wait(barrier, len(peers))
+
+    tok_copies = exchange(tok_send, tok_recv, tok_ssem, tok_rsem)
+    for out, _ in tok_copies:
+        out.start()
+    tok_recv[pl.ds(me, 1)] = tok_send[pl.ds(me, 1)]
+    grad = out_grad[...].astype(F32)
+    weighted = jnp.concatenate(
+        [(combine[:, k : k + 1] * grad).astype(BF16) for k in range(top)], 0
+    )
+    fill(grad_send, dot(choice, weighted, ((0,), (0,))))
+    grad_recv[pl.ds(me, 1)] = grad_send[pl.ds(me, 1)]
+    for load in loads[:2]:
+        load.wait()
+    for out, back in tok_copies:
+        back.wait_recv()
+    grad_copies = exchange(grad_send, grad_recv, grad_ssem, grad_rsem)
+    for out, _ in grad_copies:
+        out.start()
+
+    def mate_copy(c):
+        return pltpu.make_async_remote_copy(
+            src_ref=mate_send.at[c],
+            dst_ref=mate_recv.at[c],
+            send_sem=mate_ssem.at[c],
+            recv_sem=mate_rsem.at[c],
+            device_id=mate,
+            device_id_type=MESH,
+        )
+
+    pair = 2 * experts
+    other_chips = [lax.rem(chip + d, chips) for d in range(1, chips)]
+    for d in list(range(1, chips)) + [0]:
+        c = lax.rem(chip + d, chips)
+        for j in range(2):
+            at = pl.ds((c * 2 + j) * experts, experts)
+            x = tok_recv[at]
+            lo, hi = x[:, :CAP].reshape(rows, half), x[:, CAP:].reshape(rows, half)
+            for i, w in enumerate((gate_w, up_w)):
+                part = dot(lo, w[:half]) + dot(hi, w[half:])
+
+                @pl.when(core == j)
+                def _():
+                    own_sum[d, i] = part
+
+                @pl.when(core != j)
+                def _():
+                    mate_send[d, i] = part.astype(BF16)
+
+        mate_copy(d).start()
+
+    def cross_copy(d):
+        return pltpu.make_async_remote_copy(
+            src_ref=cross_send.at[d],
+            dst_ref=cross_recv.at[d],
+            send_sem=cross_ssem.at[d],
+            recv_sem=cross_rsem.at[d],
+            device_id={"dp": lax.rem(chip + d, chips) * 2 + core},
+            device_id_type=MESH,
+        )
+
+    for d in range(1, chips):
+        mate_copy(d).wait_recv()
+        cross_send[d] = (own_sum[d] + mate_recv[d].astype(F32)).astype(BF16)
+        cross_copy(d).start()
+    mate_copy(0).wait_recv()
+    total = own_sum[0] + mate_recv[0].astype(F32)
+    own_sum[0] = total
+    for d in range(1, chips):
+        cross_copy(d).wait_recv()
+    total = own_sum[0]
+    for d in range(1, chips):
+        total = total + cross_recv[d].astype(F32)
+    gate, up = total[0], total[1]
+    hid[pl.ds(r, 1)] = ((gate / (1.0 + jnp.exp(-gate))) * up).astype(BF16)[None]
+
+    def hid_copy(d, src, at, target, ssem, rsem):
+        return pltpu.make_async_remote_copy(
+            src_ref=hid.at[src],
+            dst_ref=hid.at[at],
+            send_sem=ssem.at[d],
+            recv_sem=rsem.at[d],
+            device_id={"dp": target},
+            device_id_type=MESH,
+        )
+
+    hid_out, hid_in = [], []
+    for d in range(1, chips):
+        ahead = lax.rem(chip + d, chips) * 2 + core
+        behind = lax.rem(chip + chips - d, chips) * 2 + core
+        hid_out.append(hid_copy(d, r, r, ahead, hid_ssem, hid_rsem))
+        hid_in.append(hid_copy(d, r, behind, ahead, hid_ssem, hid_rsem))
+    for copy in hid_out:
+        copy.start()
+    mate_r = chip * 2 + 1 - core
+    mate_out = hid_copy(0, r, r, mate_r, fwd_ssem, fwd_rsem)
+    mate_in = hid_copy(0, r, mate_r, mate_r, fwd_ssem, fwd_rsem)
+    mate_out.start()
+    loads[2].wait()
+
+    ret_copies = exchange(ret_send, ret_recv, ret_ssem, ret_rsem)
+
+    def give_back(pr):
+        out = dot(hid[pr], down_w[...], ((1,), (1,)))
+        for pe in range(experts):
+            ret_send[pr * experts + pe] = slab(out[pe * CAP : (pe + 1) * CAP])
+
+    def send_back(dr_pr, skip_self):
+        for de in range(experts):
+            if skip_self and de == 0:
+                continue
+            pe = lax.rem(e + de, experts)
+            n = dr_pr * experts + pe
+            pltpu.make_async_remote_copy(
+                src_ref=ret_send.at[n],
+                dst_ref=ret_recv.at[me],
+                send_sem=ret_ssem.at[n],
+                recv_sem=ret_rsem.at[me],
+                device_id={"expert": pe, "dp": dr_pr},
+                device_id_type=MESH,
+            ).start()
+
+    give_back(r)
+    send_back(r, True)
+    ret_recv[pl.ds(me, 1)] = ret_send[pl.ds(me, 1)]
+    mate_in.wait_recv()
+    give_back(mate_r)
+    send_back(mate_r, False)
+    forwards = []
+    for d in range(1, chips):
+        hid_in[d - 1].wait_recv()
+        behind = lax.rem(chip + chips - d, chips)
+        out = hid_copy(d, behind * 2 + core, behind * 2 + core, mate_r, fwd_ssem, fwd_rsem)
+        into = hid_copy(d, behind * 2 + core, behind * 2 + 1 - core, mate_r, fwd_ssem, fwd_rsem)
+        out.start()
+        forwards.append((out, into))
+        give_back(behind * 2 + core)
+        send_back(behind * 2 + core, False)
+    for d in range(1, chips):
+        forwards[d - 1][1].wait_recv()
+        behind = lax.rem(chip + chips - d, chips)
+        give_back(behind * 2 + 1 - core)
+        send_back(behind * 2 + 1 - core, False)
+
+    for _, back in grad_copies:
+        back.wait_recv()
+    hidden = hid[...].reshape(replicas * rows, ff)
+    for h in range(2):
+        g = grad_recv[:, h * CAP : (h + 1) * CAP].reshape(replicas * rows, half)
+        down_grad[h * half : (h + 1) * half] = dot(g, hidden, ((0,), (0,))).astype(BF16)
+
+    for _, back in ret_copies:
+        back.wait_recv()
+    for pr in range(replicas):
+        for h in range(2):
+            block = ret_recv[pr * experts : (pr + 1) * experts, h * CAP : (h + 1) * CAP]
+            got = dot(choice, block.reshape(rows, half))
+            value = combine[:, 0:1] * got[:tok_count]
+            for k in range(1, top):
+                value = value + combine[:, k : k + 1] * got[k * tok_count : (k + 1) * tok_count]
+            start = pr * width + h * half
+            mixed[:, start : start + half] = value.astype(BF16)
+
+    for copies in (tok_copies, grad_copies, ret_copies):
+        for out, _ in copies:
+            out.wait_send()
+    for d in range(chips):
+        mate_copy(d).wait_send()
+    for d in range(1, chips):
+        cross_copy(d).wait_send()
+    for copy in hid_out:
+        copy.wait_send()
+    mate_out.wait_send()
+    for out, _ in forwards:
+        out.wait_send()
+
+
+def tokens_move(tokens, out_grad, expert_ids, combine, gate_weight, up_weight, down_t):
+    experts, replicas = lax.axis_size("expert"), lax.axis_size("dp")
+    _, width, ff = gate_weight.shape
+    peers, chips, rows = experts * replicas, replicas // 2, experts * CAP
+    slabs = pltpu.VMEM((peers, 2 * CAP, width // 2), BF16)
+    dma = pltpu.SemaphoreType.DMA
+    vmem = pl.BlockSpec(memory_space=pltpu.VMEM)
+    hbm = pl.BlockSpec(memory_space=pl.ANY)
+    mixed, down_grad = pl.pallas_call(
+        functools.partial(kernel, experts, replicas),
+        out_shape=(
+            jax.ShapeDtypeStruct(tokens.shape, BF16),
+            jax.ShapeDtypeStruct((width, ff), BF16),
+        ),
+        in_specs=[vmem] * 4 + [hbm] * 3,
+        out_specs=(vmem, vmem),
+        scratch_shapes=[pltpu.VMEM((width, ff), BF16)] * 3
+        + [slabs] * 6
+        + [pltpu.VMEM((chips, 2, rows, ff), BF16)] * 4
+        + [pltpu.VMEM((chips, 2, rows, ff), F32), pltpu.VMEM((replicas, rows, ff), BF16)]
+        + [dma((3,))]
+        + [dma((peers,))] * 6
+        + [dma((chips,))] * 8,
+        compiler_params=pltpu.CompilerParams(
+            collective_id=0, has_side_effects=True, vmem_limit_bytes=40 * 1024 * 1024
+        ),
+    )(tokens, out_grad, expert_ids, combine, gate_weight[0], up_weight[0], down_t[0])
+    return mixed, down_grad[None]
+
+
+def weights_move(tokens, out_grad, expert_ids, combine, gate_weight, up_weight, down_t):
     experts = lax.axis_size("expert")
     tok_count, top_count = expert_ids.shape
     model_width = tokens.shape[1]
@@ -83,6 +426,18 @@
         P("expert", "dp", None),
     )
     out_specs = (P(("group", "expert", "dp"), None), P(("group", "expert"), "dp", None))
+
+    def per_device(*args):
+        experts, replicas = lax.axis_size("expert"), lax.axis_size("dp")
+        features, ff = args[0].shape[1], args[4].shape[2]
+        slots = experts * replicas * CAP
+        moved_tokens = slots * (3 * features // replicas + 3 * ff)
+        moved_weights = 4 * features * ff + 3 * experts * CAP * features
+        small = moved_tokens < moved_weights and slots <= 1024
+        if small and replicas % 2 == 0 and features % (256 * replicas) == 0:
+            return tokens_move(*args)
+        return weights_move(*args)
+
     return jax.shard_map(
         per_device, mesh=mesh, in_specs=in_specs, out_specs=out_specs, check_vma=False
     )

time: 149 us -> 51.8 us (0.35)
  waiting for transfers between devices: 97.9 us -> 0 us
  Pallas kernels: 0 us -> 42.7 us
  starting transfers between devices: 14.7 us -> 0 us
  between operations: 13.9 us -> 0.65 us
  matrix products: 11.5 us -> 0 us
  other arithmetic: 3.33 us -> 0 us
    all_gather x3 -> x0, waiting for transfers between devices: 56.8 us -> none  [the longest x1 27.6 us: per_device(): up_sum = add_rows(lax.all_gather(up_shard, 'dp', axis=0, tiled=True))]
    pallas_call x0 -> x1, Pallas kernels: none -> 42.7 us  [tokens_move(): pl.pallas_call(functools.partial(kernel, experts, replicas), out_shape=(j...]
    all_to_all x3 -> x0, waiting for transfers between devices: 20.9 us -> none  [the longest x1 12.1 us: per_device(): lax.all_to_all(expert_out.reshape(experts, CAP, model_width), 'expert', s...]
    reduce_scatter x1 -> x0, waiting for transfers between devices: 18.1 us -> none  [per_device(): lax.psum_scatter(lax.dot_general(grad_rows, hidden, (((0,), (0,)), ((), (...]
    all_to_all x3 -> x0, starting transfers between devices: 14.5 us -> none  [the longest x1 6.45 us: per_device(): lax.all_to_all(send_rows, 'expert', split_axis=0, concat_axis=0, tiled=True)]
    dot_general x4 -> x0, matrix products: 11.5 us -> none  [the longest x2 5.07 us: add_rows(): return jnp.dot(expert_rows, shard_piece, preferred_element_type=jnp.float32)]
    unnamed x6 -> x18, local copies, waits for them, and re-layouts: 0.86 us -> 8.18 us
    gather x3 -> x0, local copies, waits for them, and re-layouts: 3.16 us -> none  [the longest x1 1.58 us: per_device(): send_rows = padded_rows[slot_token].reshape(experts, CAP, model_width)]
  transfers between devices with their start and end apart: 7 -> 0, of which waited for: 6 -> 0; matrix products, arithmetic and copies ran while one was open for 15% -> 0% of each run, Pallas kernels for 0% -> 0%
where the time goes in v1:
time: 51.8 us; the launch traced here: 51.5 us
  Pallas kernels  42.7 us (82%)
  local copies, waits for them, and re-layouts  8.18 us (16%)
  between operations  0.65 us (1%)
    pallas_call x1, Pallas kernels, tokens_move(): pl.pallas_call(functools.partial(kernel, experts, replicas), out_shape=(j...  42.7 us
    unnamed x18, local copies, waits for them, and re-layouts  8.18 us

profile of v1, /device:TPU:0, one launch (start us, length us, event | category | flops | bytes accessed | tf_op | source)
XLA Modules:
  0.0 51.5 jit_solution(15228360490929498591)
XLA Ops:
  0.6 0.0 copy-start.5
  0.6 0.7 %copy-done.5 = s32[32,2]{0,1:T(2,128)S(1)} copy-done((s32[32,2]{0,1:T(2,128)S(1)}, s32[32,2]{0,1:T(2,128)}, u32[]{:S(2)}) %copy-start.5) | copy-done | bytes 280
  1.3 0.0 copy-start.6
  1.3 0.1 copy.9.expert_ids
  1.4 0.6 %copy-done.6 = f32[32,2]{0,1:T(2,128)S(1)} copy-done((f32[32,2]{0,1:T(2,128)S(1)}, f32[32,2]{0,1:T(2,128)}, u32[]{:S(2)}) %copy-start.6) | copy-done | bytes 280
  2.0 0.1 copy.10.combine
  2.1 0.0 copy-start
  2.1 1.1 %copy-done = bf16[1,512,768]{2,1,0:T(8,128)(2,1)S(1)} copy-done((bf16[1,512,768]{2,1,0:T(8,128)(2,1)S(1)}, bf16[1,512,768]{2,1,0:T(8,128)(2,1)}, u32[]{:S(2)}) %copy-start) | copy-done | bytes 786456
  3.2 0.0 copy-start.1
  3.2 1.1 %copy-done.1 = bf16[1,512,768]{2,1,0:T(8,128)(2,1)S(1)} copy-done((bf16[1,512,768]{2,1,0:T(8,128)(2,1)S(1)}, bf16[1,512,768]{2,1,0:T(8,128)(2,1)}, u32[]{:S(2)}) %copy-start.1) | copy-done | bytes 786456
  4.3 0.0 copy-start.2
  4.3 1.1 %copy-done.2 = bf16[1,512,768]{2,1,0:T(8,128)(2,1)S(1)} copy-done((bf16[1,512,768]{2,1,0:T(8,128)(2,1)S(1)}, bf16[1,512,768]{2,1,0:T(8,128)(2,1)}, u32[]{:S(2)}) %copy-start.2) | copy-done | bytes 786456
  5.5 0.0 copy-start.3
  5.5 0.9 %copy-done.3 = bf16[32,2048]{1,0:T(8,128)(2,1)S(1)} copy-done((bf16[32,2048]{1,0:T(8,128)(2,1)S(1)}, bf16[32,2048]{1,0:T(8,128)(2,1)}, u32[]{:S(2)}) %copy-start.3) | copy-done | bytes 131096
  6.4 0.0 copy-start.4
  6.4 0.9 %copy-done.4 = bf16[32,2048]{1,0:T(8,128)(2,1)S(1)} copy-done((bf16[32,2048]{1,0:T(8,128)(2,1)S(1)}, bf16[32,2048]{1,0:T(8,128)(2,1)}, u32[]{:S(2)}) %copy-start.4) | copy-done | bytes 131096
  7.3 42.7 %shard_map.86 = (bf16[32,2048]{1,0:T(8,128)(2,1)S(1)}, bf16[512,768]{1,0:T(8,128)(2,1)S(1)}) custom-call(bf16[32,2048]{1,0:T(8,128)(2,1)S(1)} %copy-done.3, bf16[32,2048]{1,0:T(8,128)(2,1)S(1)} %copy-done.4, s32[32,2]{1,0:T(8,128)S(1)} %copy.9.expert_ids, f32[32,2]{1,0:T(8,128)S(1)} %copy.10.combine, bf16[512,768]{1,0:T(8,128)(2,1)S(1)} %bitcast.5, ...), custom_call_target="tpu_custom_call" | custom-call | tf_op jit(solution)/shard_map/pallas_call | solution.py:330
  50.0 0.7 %copy.13 = bf16[32,2048]{1,0:T(8,128)(2,1)} copy(bf16[32,2048]{1,0:T(8,128)(2,1)S(1)} %get-tuple-element.8) | data formatting | bytes 262144
  50.6 0.9 %copy.14 = bf16[1,512,768]{2,1,0:T(8,128)(2,1)} copy(bf16[1,512,768]{2,1,0:T(8,128)(2,1)S(1)} %bitcast.4) | data formatting | bytes 1572864
Async XLA Ops:
  0.6 0.7 %copy-start.5 = (s32[32,2]{0,1:T(2,128)S(1)}, s32[32,2]{0,1:T(2,128)}, u32[]{:S(2)}) copy-start(s32[32,2]{0,1:T(2,128)} %param.9) | copy-start | bytes 772
  1.3 0.7 %copy-start.6 = (f32[32,2]{0,1:T(2,128)S(1)}, f32[32,2]{0,1:T(2,128)}, u32[]{:S(2)}) copy-start(f32[32,2]{0,1:T(2,128)} %param.10) | copy-start | bytes 772
  2.1 1.1 %copy-start = (bf16[1,512,768]{2,1,0:T(8,128)(2,1)S(1)}, bf16[1,512,768]{2,1,0:T(8,128)(2,1)}, u32[]{:S(2)}) copy-start(bf16[1,512,768]{2,1,0:T(8,128)(2,1)} %param.11) | copy-start | bytes 2359300
  3.2 1.1 %copy-start.1 = (bf16[1,512,768]{2,1,0:T(8,128)(2,1)S(1)}, bf16[1,512,768]{2,1,0:T(8,128)(2,1)}, u32[]{:S(2)}) copy-start(bf16[1,512,768]{2,1,0:T(8,128)(2,1)} %param.12) | copy-start | bytes 2359300
  4.3 1.1 %copy-start.2 = (bf16[1,512,768]{2,1,0:T(8,128)(2,1)S(1)}, bf16[1,512,768]{2,1,0:T(8,128)(2,1)}, u32[]{:S(2)}) copy-start(bf16[1,512,768]{2,1,0:T(8,128)(2,1)} %param.13) | copy-start | bytes 2359300
  5.5 0.9 %copy-start.3 = (bf16[32,2048]{1,0:T(8,128)(2,1)S(1)}, bf16[32,2048]{1,0:T(8,128)(2,1)}, u32[]{:S(2)}) copy-start(bf16[32,2048]{1,0:T(8,128)(2,1)} %tokens.1) | copy-start | bytes 393220
  6.4 0.9 %copy-start.4 = (bf16[32,2048]{1,0:T(8,128)(2,1)S(1)}, bf16[32,2048]{1,0:T(8,128)(2,1)}, u32[]{:S(2)}) copy-start(bf16[32,2048]{1,0:T(8,128)(2,1)} %out_grad.1) | copy-start | bytes 393220

commit v2 on v1

--- a/solution.py
+++ b/solution.py
@@ -20,10 +20,10 @@
 def kernel(
     experts,
     replicas,
-    tokens,
-    out_grad,
-    expert_ids,
-    combine,
+    tokens_hbm,
+    out_grad_hbm,
+    ids_hbm,
+    combine_hbm,
     gate_hbm,
     up_hbm,
     down_hbm,
@@ -32,6 +32,10 @@
     gate_w,
     up_w,
     down_w,
+    tokens,
+    out_grad,
+    expert_ids,
+    combine,
     tok_send,
     tok_recv,
     grad_send,
@@ -74,7 +78,17 @@
 
     loads = [
         pltpu.make_async_copy(src, dst, load_sem.at[i])
-        for i, (src, dst) in enumerate(((gate_hbm, gate_w), (up_hbm, up_w), (down_hbm, down_w)))
+        for i, (src, dst) in enumerate(
+            (
+                (ids_hbm, expert_ids),
+                (tokens_hbm, tokens),
+                (combine_hbm, combine),
+                (out_grad_hbm, out_grad),
+                (gate_hbm, gate_w),
+                (up_hbm, up_w),
+                (down_hbm, down_w),
+            )
+        )
     ]
     for load in loads:
         load.start()
@@ -125,36 +139,41 @@
                 )
 
     tok_count = tokens.shape[0]
-    top = expert_ids.shape[1]
-    column = lax.broadcasted_iota(jnp.int32, (tok_count, rows), 1)
-    owner = jnp.zeros((tok_count, rows), jnp.int32)
+    top = expert_ids.shape[0]
+    line = lax.broadcasted_iota(jnp.int32, (rows, tok_count), 0)
+    owner = jnp.zeros((rows, tok_count), jnp.int32)
     for j in range(1, experts):
-        owner = owner + (column >= j * CAP).astype(jnp.int32)
-    place = (column - owner * CAP).astype(F32)
-    picks = [(expert_ids[:, k : k + 1] == owner).astype(F32) for k in range(top)]
+        owner = owner + (line >= j * CAP).astype(jnp.int32)
+    place = (line - owner * CAP).astype(F32)
+    token_down = lax.broadcasted_iota(jnp.int32, (tok_count, tok_count), 0)
+    token_along = lax.broadcasted_iota(jnp.int32, (tok_count, tok_count), 1)
+    earlier = (token_down < token_along).astype(F32).astype(BF16)
+    loads[0].wait()
+    picks = [(expert_ids[k : k + 1, :] == owner).astype(F32) for k in range(top)]
     named = functools.reduce(jnp.add, picks)
-    earlier = (
-        lax.broadcasted_iota(jnp.int32, (tok_count, tok_count), 0)
-        > lax.broadcasted_iota(jnp.int32, (tok_count, tok_count), 1)
-    ).astype(F32)
-    slot = dot(earlier.astype(BF16), named.astype(BF16))
-    here = jnp.where(slot == place, 1.0, 0.0)
-    choice = jnp.concatenate([pick * here for pick in picks], 0).astype(BF16)
+    here = jnp.where(dot(named.astype(BF16), earlier) == place, 1.0, 0.0)
+    picks = [pick * here for pick in picks]
     either = (named * here).astype(BF16)
-    fill(tok_send, dot(either, tokens[...], ((0,), (0,))))
+    loads[1].wait()
+    fill(tok_send, dot(either, tokens[...]))
     pl.semaphore_wait(barrier, len(peers))
 
     tok_copies = exchange(tok_send, tok_recv, tok_ssem, tok_rsem)
     for out, _ in tok_copies:
         out.start()
     tok_recv[pl.ds(me, 1)] = tok_send[pl.ds(me, 1)]
-    grad = out_grad[...].astype(F32)
-    weighted = jnp.concatenate(
-        [(combine[:, k : k + 1] * grad).astype(BF16) for k in range(top)], 0
-    )
-    fill(grad_send, dot(choice, weighted, ((0,), (0,))))
+    loads[2].wait()
+    loads[3].wait()
+    slot_weight = jnp.zeros((rows, 1), F32)
+    weights = []
+    for k in range(top):
+        row = combine[k : k + 1, :]
+        slot_weight = slot_weight + jnp.sum(picks[k] * row, 1, keepdims=True)
+        weights.append(jnp.sum(jnp.where(token_down == token_along, row, 0.0), 1, keepdims=True))
+    fill(grad_send, slot_weight * dot(either, out_grad[...]))
+    picks = [pick.astype(BF16) for pick in picks]
     grad_recv[pl.ds(me, 1)] = grad_send[pl.ds(me, 1)]
-    for load in loads[:2]:
+    for load in loads[4:6]:
         load.wait()
     for out, back in tok_copies:
         back.wait_recv()
@@ -240,7 +259,7 @@
     mate_out = hid_copy(0, r, r, mate_r, fwd_ssem, fwd_rsem)
     mate_in = hid_copy(0, r, mate_r, mate_r, fwd_ssem, fwd_rsem)
     mate_out.start()
-    loads[2].wait()
+    loads[6].wait()
 
     ret_copies = exchange(ret_send, ret_recv, ret_ssem, ret_rsem)
 
@@ -298,10 +317,10 @@
     for pr in range(replicas):
         for h in range(2):
             block = ret_recv[pr * experts : (pr + 1) * experts, h * CAP : (h + 1) * CAP]
-            got = dot(choice, block.reshape(rows, half))
-            value = combine[:, 0:1] * got[:tok_count]
+            block = block.reshape(rows, half)
+            value = weights[0] * dot(picks[0], block, ((0,), (0,)))
             for k in range(1, top):
-                value = value + combine[:, k : k + 1] * got[k * tok_count : (k + 1) * tok_count]
+                value = value + weights[k] * dot(picks[k], block, ((0,), (0,)))
             start = pr * width + h * half
             mixed[:, start : start + half] = value.astype(BF16)
 
@@ -322,6 +341,7 @@
 def tokens_move(tokens, out_grad, expert_ids, combine, gate_weight, up_weight, down_t):
     experts, replicas = lax.axis_size("expert"), lax.axis_size("dp")
     _, width, ff = gate_weight.shape
+    top = expert_ids.shape[1]
     peers, chips, rows = experts * replicas, replicas // 2, experts * CAP
     slabs = pltpu.VMEM((peers, 2 * CAP, width // 2), BF16)
     dma = pltpu.SemaphoreType.DMA
@@ -333,19 +353,22 @@
             jax.ShapeDtypeStruct(tokens.shape, BF16),
             jax.ShapeDtypeStruct((width, ff), BF16),
         ),
-        in_specs=[vmem] * 4 + [hbm] * 3,
+        in_specs=[hbm] * 7,
         out_specs=(vmem, vmem),
         scratch_shapes=[pltpu.VMEM((width, ff), BF16)] * 3
+        + [pltpu.VMEM(tokens.shape, BF16)] * 2
+        + [pltpu.VMEM((top, tokens.shape[0]), jnp.int32)]
+        + [pltpu.VMEM((top, tokens.shape[0]), F32)]
         + [slabs] * 6
         + [pltpu.VMEM((chips, 2, rows, ff), BF16)] * 4
         + [pltpu.VMEM((chips, 2, rows, ff), F32), pltpu.VMEM((replicas, rows, ff), BF16)]
-        + [dma((3,))]
+        + [dma((7,))]
         + [dma((peers,))] * 6
         + [dma((chips,))] * 8,
         compiler_params=pltpu.CompilerParams(
-            collective_id=0, has_side_effects=True, vmem_limit_bytes=40 * 1024 * 1024
+            collective_id=0, has_side_effects=True, vmem_limit_bytes=60 * 1024 * 1024
         ),
-    )(tokens, out_grad, expert_ids, combine, gate_weight[0], up_weight[0], down_t[0])
+    )(tokens, out_grad, expert_ids.T, combine.T, gate_weight[0], up_weight[0], down_t[0])
     return mixed, down_grad[None]
 
 

time: 51.8 us -> 48 us (0.927)
  local copies, waits for them, and re-layouts: 8.18 us -> 3.63 us
  Pallas kernels: 42.7 us -> 43.6 us
    unnamed x18 -> x2, local copies, waits for them, and re-layouts: 8.18 us -> 3.63 us
    pallas_call x1, Pallas kernels: 42.7 us -> 43.6 us  [tokens_move(): pl.pallas_call(functools.partial(kernel, experts, replicas), out_shape=(j...]
where the time goes in v2:
time: 48 us; the launch traced here: 47.8 us
  Pallas kernels  43.6 us (91%)
  local copies, waits for them, and re-layouts  3.63 us (8%)
  between operations  0.64 us (1%)
    pallas_call x1, Pallas kernels, tokens_move(): pl.pallas_call(functools.partial(kernel, experts, replicas), out_shape=(j...  43.6 us
    unnamed x2, local copies, waits for them, and re-layouts  3.63 us

profile of v2, /device:TPU:0, one launch (start us, length us, event | category | flops | bytes accessed | tf_op | source)
XLA Modules:
  0.0 47.8 jit_solution(11316049882327699514)
XLA Ops:
  0.6 43.6 %shard_map.86 = (bf16[32,2048]{1,0:T(8,128)(2,1)}, bf16[512,768]{1,0:T(8,128)(2,1)}) custom-call(bf16[32,2048]{1,0:T(8,128)(2,1)} %tokens_hbm.1, bf16[32,2048]{1,0:T(8,128)(2,1)} %out_grad_hbm.1, s32[2,32]{1,0:T(2,128)} %bitcast.10, f32[2,32]{1,0:T(2,128)} %bitcast.11, bf16[512,768]{1,0:T(8,128)(2,1)} %bitcast.7, bf16[512,768]{1,0:T(8,128)(2,1)} %bitcast.8, ...), custom_call_target="tpu_custom_call" | custom-call | tf_op jit(solution)/shard_map/pallas_call | solution.py:350
  44.2 1.6 %copy.11 = bf16[32,2048]{1,0:T(8,128)(2,1)} copy(bf16[32,2048]{1,0:T(8,128)(2,1)} %get-tuple-element.8) | data formatting | bytes 262144
  45.8 2.1 %copy.12 = bf16[1,512,768]{2,1,0:T(8,128)(2,1)} copy(bf16[1,512,768]{2,1,0:T(8,128)(2,1)} %bitcast.6) | data formatting | bytes 1572864

commit v3 on v2

--- a/solution.py
+++ b/solution.py
@@ -27,8 +27,8 @@
     gate_hbm,
     up_hbm,
     down_hbm,
-    mixed,
-    down_grad,
+    mixed_hbm,
+    down_grad_hbm,
     gate_w,
     up_w,
     down_w,
@@ -36,6 +36,8 @@
     out_grad,
     expert_ids,
     combine,
+    mixed,
+    down_grad,
     tok_send,
     tok_recv,
     grad_send,
@@ -49,6 +51,7 @@
     own_sum,
     hid,
     load_sem,
+    store_sem,
     tok_ssem,
     tok_rsem,
     grad_ssem,
@@ -93,12 +96,16 @@
     for load in loads:
         load.start()
 
-    peers = []
-    for dr in range(replicas):
-        for de in range(experts):
-            if dr or de:
-                pe, pr = lax.rem(e + de, experts), lax.rem(r + dr, replicas)
-                peers.append((pe, pr, pr * experts + pe))
+    peers, chip_peers = [], {}
+    for d in list(range(1, chips)) + [0]:
+        chip_peers[d] = []
+        for dc in range(2):
+            for de in range(experts):
+                if d or dc or de:
+                    pe = lax.rem(e + de, experts)
+                    pr = lax.rem(chip + d, chips) * 2 + lax.rem(core + dc, 2)
+                    chip_peers[d].append(len(peers))
+                    peers.append((pe, pr, pr * experts + pe))
     barrier = pltpu.get_barrier_semaphore()
     for pe, pr, _ in peers:
         pl.semaphore_signal(barrier, inc=1, device_id={"expert": pe, "dp": pr}, device_id_type=MESH)
@@ -175,11 +182,7 @@
     grad_recv[pl.ds(me, 1)] = grad_send[pl.ds(me, 1)]
     for load in loads[4:6]:
         load.wait()
-    for out, back in tok_copies:
-        back.wait_recv()
     grad_copies = exchange(grad_send, grad_recv, grad_ssem, grad_rsem)
-    for out, _ in grad_copies:
-        out.start()
 
     def mate_copy(c):
         return pltpu.make_async_remote_copy(
@@ -191,27 +194,6 @@
             device_id_type=MESH,
         )
 
-    pair = 2 * experts
-    other_chips = [lax.rem(chip + d, chips) for d in range(1, chips)]
-    for d in list(range(1, chips)) + [0]:
-        c = lax.rem(chip + d, chips)
-        for j in range(2):
-            at = pl.ds((c * 2 + j) * experts, experts)
-            x = tok_recv[at]
-            lo, hi = x[:, :CAP].reshape(rows, half), x[:, CAP:].reshape(rows, half)
-            for i, w in enumerate((gate_w, up_w)):
-                part = dot(lo, w[:half]) + dot(hi, w[half:])
-
-                @pl.when(core == j)
-                def _():
-                    own_sum[d, i] = part
-
-                @pl.when(core != j)
-                def _():
-                    mate_send[d, i] = part.astype(BF16)
-
-        mate_copy(d).start()
-
     def cross_copy(d):
         return pltpu.make_async_remote_copy(
             src_ref=cross_send.at[d],
@@ -222,13 +204,35 @@
             device_id_type=MESH,
         )
 
-    for d in range(1, chips):
+    for d in list(range(1, chips)) + [0]:
+        for i in chip_peers[d]:
+            tok_copies[i][1].wait_recv()
+        if d == 0:
+            for out, _ in grad_copies:
+                out.start()
+        at = pl.ds(lax.rem(chip + d, chips) * 2 * experts, 2 * experts)
+        x = tok_recv[at]
+        lo, hi = x[:, :CAP].reshape(2 * rows, half), x[:, CAP:].reshape(2 * rows, half)
+        for i, w in enumerate((gate_w, up_w)):
+            part = dot(lo, w[:half]) + dot(hi, w[half:])
+            for j in range(2):
+                share = part[j * rows : (j + 1) * rows]
+
+                @pl.when(core == j)
+                def _():
+                    own_sum[d, i] = share
+
+                @pl.when(core != j)
+                def _():
+                    mate_send[d, i] = share.astype(BF16)
+
+        mate_copy(d).start()
         mate_copy(d).wait_recv()
-        cross_send[d] = (own_sum[d] + mate_recv[d].astype(F32)).astype(BF16)
-        cross_copy(d).start()
-    mate_copy(0).wait_recv()
-    total = own_sum[0] + mate_recv[0].astype(F32)
-    own_sum[0] = total
+        if d:
+            cross_send[d] = (own_sum[d] + mate_recv[d].astype(F32)).astype(BF16)
+            cross_copy(d).start()
+        else:
+            own_sum[0] = own_sum[0] + mate_recv[0].astype(F32)
     for d in range(1, chips):
         cross_copy(d).wait_recv()
     total = own_sum[0]
@@ -312,6 +316,8 @@
         g = grad_recv[:, h * CAP : (h + 1) * CAP].reshape(replicas * rows, half)
         down_grad[h * half : (h + 1) * half] = dot(g, hidden, ((0,), (0,))).astype(BF16)
 
+    store_grad = pltpu.make_async_copy(down_grad, down_grad_hbm, store_sem.at[0])
+    store_grad.start()
     for _, back in ret_copies:
         back.wait_recv()
     for pr in range(replicas):
@@ -324,6 +330,8 @@
             start = pr * width + h * half
             mixed[:, start : start + half] = value.astype(BF16)
 
+    store_mixed = pltpu.make_async_copy(mixed, mixed_hbm, store_sem.at[1])
+    store_mixed.start()
     for copies in (tok_copies, grad_copies, ret_copies):
         for out, _ in copies:
             out.wait_send()
@@ -336,6 +344,8 @@
     mate_out.wait_send()
     for out, _ in forwards:
         out.wait_send()
+    store_grad.wait()
+    store_mixed.wait()
 
 
 def tokens_move(tokens, out_grad, expert_ids, combine, gate_weight, up_weight, down_t):
@@ -345,7 +355,6 @@
     peers, chips, rows = experts * replicas, replicas // 2, experts * CAP
     slabs = pltpu.VMEM((peers, 2 * CAP, width // 2), BF16)
     dma = pltpu.SemaphoreType.DMA
-    vmem = pl.BlockSpec(memory_space=pltpu.VMEM)
     hbm = pl.BlockSpec(memory_space=pl.ANY)
     mixed, down_grad = pl.pallas_call(
         functools.partial(kernel, experts, replicas),
@@ -354,15 +363,16 @@
             jax.ShapeDtypeStruct((width, ff), BF16),
         ),
         in_specs=[hbm] * 7,
-        out_specs=(vmem, vmem),
+        out_specs=(hbm, hbm),
         scratch_shapes=[pltpu.VMEM((width, ff), BF16)] * 3
         + [pltpu.VMEM(tokens.shape, BF16)] * 2
         + [pltpu.VMEM((top, tokens.shape[0]), jnp.int32)]
         + [pltpu.VMEM((top, tokens.shape[0]), F32)]
+        + [pltpu.VMEM(tokens.shape, BF16), pltpu.VMEM((width, ff), BF16)]
         + [slabs] * 6
         + [pltpu.VMEM((chips, 2, rows, ff), BF16)] * 4
         + [pltpu.VMEM((chips, 2, rows, ff), F32), pltpu.VMEM((replicas, rows, ff), BF16)]
-        + [dma((7,))]
+        + [dma((7,)), dma((2,))]
         + [dma((peers,))] * 6
         + [dma((chips,))] * 8,
         compiler_params=pltpu.CompilerParams(

time: 48 us -> 44.5 us (0.927)
  Pallas kernels: 43.6 us -> 40 us
    pallas_call x1, Pallas kernels: 43.6 us -> 40 us  [tokens_move(): pl.pallas_call(functools.partial(kernel, experts, replicas), out_shape=(j...]
where the time goes in v3:
time: 44.5 us; the launch traced here: 44.3 us
  Pallas kernels  40 us (90%)
  local copies, waits for them, and re-layouts  3.63 us (8%)
  between operations  0.64 us (1%)
    pallas_call x1, Pallas kernels, tokens_move(): pl.pallas_call(functools.partial(kernel, experts, replicas), out_shape=(j...  40 us
    unnamed x2, local copies, waits for them, and re-layouts  3.63 us

profile of v3, /device:TPU:0, one launch (start us, length us, event | category | flops | bytes accessed | tf_op | source)
XLA Modules:
  0.0 44.3 jit_solution(13077762565203215736)
XLA Ops:
  0.6 40.0 %shard_map.86 = (bf16[32,2048]{1,0:T(8,128)(2,1)}, bf16[512,768]{1,0:T(8,128)(2,1)}) custom-call(bf16[32,2048]{1,0:T(8,128)(2,1)} %tokens_hbm.1, bf16[32,2048]{1,0:T(8,128)(2,1)} %out_grad_hbm.1, s32[2,32]{1,0:T(2,128)} %bitcast.10, f32[2,32]{1,0:T(2,128)} %bitcast.11, bf16[512,768]{1,0:T(8,128)(2,1)} %bitcast.7, bf16[512,768]{1,0:T(8,128)(2,1)} %bitcast.8, ...), custom_call_target="tpu_custom_call" | custom-call | tf_op jit(solution)/shard_map/pallas_call | solution.py:359
  40.6 1.6 %copy.11 = bf16[32,2048]{1,0:T(8,128)(2,1)} copy(bf16[32,2048]{1,0:T(8,128)(2,1)} %get-tuple-element.8) | data formatting | bytes 262144
  42.2 2.1 %copy.12 = bf16[1,512,768]{2,1,0:T(8,128)(2,1)} copy(bf16[1,512,768]{2,1,0:T(8,128)(2,1)} %bitcast.6) | data formatting | bytes 1572864

commit v4 on v3

--- a/solution.py
+++ b/solution.py
@@ -184,22 +184,22 @@
         load.wait()
     grad_copies = exchange(grad_send, grad_recv, grad_ssem, grad_rsem)
 
-    def mate_copy(c):
+    def mate_copy(c, i):
         return pltpu.make_async_remote_copy(
-            src_ref=mate_send.at[c],
-            dst_ref=mate_recv.at[c],
-            send_sem=mate_ssem.at[c],
-            recv_sem=mate_rsem.at[c],
+            src_ref=mate_send.at[c, i],
+            dst_ref=mate_recv.at[c, i],
+            send_sem=mate_ssem.at[c, i],
+            recv_sem=mate_rsem.at[c, i],
             device_id=mate,
             device_id_type=MESH,
         )
 
-    def cross_copy(d):
+    def cross_copy(d, i):
         return pltpu.make_async_remote_copy(
-            src_ref=cross_send.at[d],
-            dst_ref=cross_recv.at[d],
-            send_sem=cross_ssem.at[d],
-            recv_sem=cross_rsem.at[d],
+            src_ref=cross_send.at[d, i],
+            dst_ref=cross_recv.at[d, i],
+            send_sem=cross_ssem.at[d, i],
+            recv_sem=cross_rsem.at[d, i],
             device_id={"dp": lax.rem(chip + d, chips) * 2 + core},
             device_id_type=MESH,
         )
@@ -208,8 +208,11 @@
         for i in chip_peers[d]:
             tok_copies[i][1].wait_recv()
         if d == 0:
-            for out, _ in grad_copies:
-                out.start()
+            for i in chip_peers[0]:
+                grad_copies[i][0].start()
+            for q in range(1, chips):
+                for i in chip_peers[q]:
+                    grad_copies[i][0].start()
         at = pl.ds(lax.rem(chip + d, chips) * 2 * experts, 2 * experts)
         x = tok_recv[at]
         lo, hi = x[:, :CAP].reshape(2 * rows, half), x[:, CAP:].reshape(2 * rows, half)
@@ -226,15 +229,18 @@
                 def _():
                     mate_send[d, i] = share.astype(BF16)
 
-        mate_copy(d).start()
-        mate_copy(d).wait_recv()
-        if d:
-            cross_send[d] = (own_sum[d] + mate_recv[d].astype(F32)).astype(BF16)
-            cross_copy(d).start()
-        else:
-            own_sum[0] = own_sum[0] + mate_recv[0].astype(F32)
-    for d in range(1, chips):
-        cross_copy(d).wait_recv()
+            mate_copy(d, i).start()
+
+        for i in range(2):
+            mate_copy(d, i).wait_recv()
+            if d:
+                cross_send[d, i] = (own_sum[d, i] + mate_recv[d, i].astype(F32)).astype(BF16)
+                cross_copy(d, i).start()
+            else:
+                own_sum[0, i] = own_sum[0, i] + mate_recv[0, i].astype(F32)
+    for d in range(1, chips):
+        for i in range(2):
+            cross_copy(d, i).wait_recv()
     total = own_sum[0]
     for d in range(1, chips):
         total = total + cross_recv[d].astype(F32)
@@ -318,27 +324,42 @@
 
     store_grad = pltpu.make_async_copy(down_grad, down_grad_hbm, store_sem.at[0])
     store_grad.start()
-    for _, back in ret_copies:
-        back.wait_recv()
-    for pr in range(replicas):
+    arrivals = [r, mate_r]
+    for d in range(1, chips):
+        arrivals.append(lax.rem(chip + chips - d, chips) * 2 + core)
+    for d in range(1, chips):
+        arrivals.append(lax.rem(chip + chips - d, chips) * 2 + 1 - core)
+    for number, pr in enumerate(arrivals):
+        for de in range(1 if number == 0 else 0, experts):
+            n = pr * experts + lax.rem(e + de, experts)
+            pltpu.make_async_remote_copy(
+                src_ref=ret_send.at[n],
+                dst_ref=ret_recv.at[n],
+                send_sem=ret_ssem.at[n],
+                recv_sem=ret_rsem.at[n],
+                device_id={"expert": lax.rem(e + de, experts), "dp": pr},
+                device_id_type=MESH,
+            ).wait_recv()
+        arrived = ret_recv[pl.ds(pr * experts, experts)]
         for h in range(2):
-            block = ret_recv[pr * experts : (pr + 1) * experts, h * CAP : (h + 1) * CAP]
+            block = arrived[:, h * CAP : (h + 1) * CAP]
             block = block.reshape(rows, half)
             value = weights[0] * dot(picks[0], block, ((0,), (0,)))
             for k in range(1, top):
                 value = value + weights[k] * dot(picks[k], block, ((0,), (0,)))
-            start = pr * width + h * half
-            mixed[:, start : start + half] = value.astype(BF16)
+            start = pl.multiple_of(pr * width + h * half, 128)
+            mixed[:, pl.ds(start, half)] = value.astype(BF16)
 
     store_mixed = pltpu.make_async_copy(mixed, mixed_hbm, store_sem.at[1])
     store_mixed.start()
     for copies in (tok_copies, grad_copies, ret_copies):
         for out, _ in copies:
             out.wait_send()
-    for d in range(chips):
-        mate_copy(d).wait_send()
-    for d in range(1, chips):
-        cross_copy(d).wait_send()
+    for i in range(2):
+        for d in range(chips):
+            mate_copy(d, i).wait_send()
+        for d in range(1, chips):
+            cross_copy(d, i).wait_send()
     for copy in hid_out:
         copy.wait_send()
     mate_out.wait_send()
@@ -374,7 +395,8 @@
         + [pltpu.VMEM((chips, 2, rows, ff), F32), pltpu.VMEM((replicas, rows, ff), BF16)]
         + [dma((7,)), dma((2,))]
         + [dma((peers,))] * 6
-        + [dma((chips,))] * 8,
+        + [dma((chips, 2))] * 4
+        + [dma((chips,))] * 4,
         compiler_params=pltpu.CompilerParams(
             collective_id=0, has_side_effects=True, vmem_limit_bytes=60 * 1024 * 1024
         ),

time: 44.5 us -> 43.1 us (0.969)
  Pallas kernels: 40 us -> 38.6 us
    pallas_call x1, Pallas kernels: 40 us -> 38.6 us  [tokens_move(): pl.pallas_call(functools.partial(kernel, experts, replicas), out_shape=(j...]
where the time goes in v4:
time: 43.1 us; the launch traced here: 42.9 us
  Pallas kernels  38.6 us (90%)
  local copies, waits for them, and re-layouts  3.63 us (8%)
  between operations  0.64 us (1%)
    pallas_call x1, Pallas kernels, tokens_move(): pl.pallas_call(functools.partial(kernel, experts, replicas), out_shape=(j...  38.6 us
    unnamed x2, local copies, waits for them, and re-layouts  3.63 us

profile of v4, /device:TPU:0, one launch (start us, length us, event | category | flops | bytes accessed | tf_op | source)
XLA Modules:
  0.0 42.9 jit_solution(15001296684035598077)
XLA Ops:
  0.6 38.6 %shard_map.86 = (bf16[32,2048]{1,0:T(8,128)(2,1)}, bf16[512,768]{1,0:T(8,128)(2,1)}) custom-call(bf16[32,2048]{1,0:T(8,128)(2,1)} %tokens_hbm.1, bf16[32,2048]{1,0:T(8,128)(2,1)} %out_grad_hbm.1, s32[2,32]{1,0:T(2,128)} %bitcast.10, f32[2,32]{1,0:T(2,128)} %bitcast.11, bf16[512,768]{1,0:T(8,128)(2,1)} %bitcast.7, bf16[512,768]{1,0:T(8,128)(2,1)} %bitcast.8, ...), custom_call_target="tpu_custom_call" | custom-call | tf_op jit(solution)/shard_map/pallas_call | solution.py:380
  39.3 1.6 %copy.11 = bf16[32,2048]{1,0:T(8,128)(2,1)} copy(bf16[32,2048]{1,0:T(8,128)(2,1)} %get-tuple-element.8) | data formatting | bytes 262144
  40.9 2.1 %copy.12 = bf16[1,512,768]{2,1,0:T(8,128)(2,1)} copy(bf16[1,512,768]{2,1,0:T(8,128)(2,1)} %bitcast.6) | data formatting | bytes 1572864

commit v5 on v4

--- a/solution.py
+++ b/solution.py
@@ -27,8 +27,8 @@
     gate_hbm,
     up_hbm,
     down_hbm,
-    mixed_hbm,
-    down_grad_hbm,
+    mixed,
+    down_grad,
     gate_w,
     up_w,
     down_w,
@@ -36,8 +36,6 @@
     out_grad,
     expert_ids,
     combine,
-    mixed,
-    down_grad,
     tok_send,
     tok_recv,
     grad_send,
@@ -51,7 +49,6 @@
     own_sum,
     hid,
     load_sem,
-    store_sem,
     tok_ssem,
     tok_rsem,
     grad_ssem,
@@ -93,7 +90,7 @@
             )
         )
     ]
-    for load in loads:
+    for load in loads[:4]:
         load.start()
 
     peers, chip_peers = [], {}
@@ -109,6 +106,9 @@
     barrier = pltpu.get_barrier_semaphore()
     for pe, pr, _ in peers:
         pl.semaphore_signal(barrier, inc=1, device_id={"expert": pe, "dp": pr}, device_id_type=MESH)
+
+    for load in loads[4:]:
+        load.start()
 
     def exchange(src, dst, ssem, rsem):
         copies = []
@@ -322,8 +322,6 @@
         g = grad_recv[:, h * CAP : (h + 1) * CAP].reshape(replicas * rows, half)
         down_grad[h * half : (h + 1) * half] = dot(g, hidden, ((0,), (0,))).astype(BF16)
 
-    store_grad = pltpu.make_async_copy(down_grad, down_grad_hbm, store_sem.at[0])
-    store_grad.start()
     arrivals = [r, mate_r]
     for d in range(1, chips):
         arrivals.append(lax.rem(chip + chips - d, chips) * 2 + core)
@@ -350,8 +348,6 @@
             start = pl.multiple_of(pr * width + h * half, 128)
             mixed[:, pl.ds(start, half)] = value.astype(BF16)
 
-    store_mixed = pltpu.make_async_copy(mixed, mixed_hbm, store_sem.at[1])
-    store_mixed.start()
     for copies in (tok_copies, grad_copies, ret_copies):
         for out, _ in copies:
             out.wait_send()
@@ -365,8 +361,6 @@
     mate_out.wait_send()
     for out, _ in forwards:
         out.wait_send()
-    store_grad.wait()
-    store_mixed.wait()
 
 
 def tokens_move(tokens, out_grad, expert_ids, combine, gate_weight, up_weight, down_t):
@@ -380,20 +374,19 @@
     mixed, down_grad = pl.pallas_call(
         functools.partial(kernel, experts, replicas),
         out_shape=(
-            jax.ShapeDtypeStruct(tokens.shape, BF16),
-            jax.ShapeDtypeStruct((width, ff), BF16),
+            pltpu.VMEM(tokens.shape, BF16),
+            pltpu.VMEM((width, ff), BF16),
         ),
         in_specs=[hbm] * 7,
-        out_specs=(hbm, hbm),
+        out_specs=(pl.BlockSpec(memory_space=pltpu.VMEM),) * 2,
         scratch_shapes=[pltpu.VMEM((width, ff), BF16)] * 3
         + [pltpu.VMEM(tokens.shape, BF16)] * 2
         + [pltpu.VMEM((top, tokens.shape[0]), jnp.int32)]
         + [pltpu.VMEM((top, tokens.shape[0]), F32)]
-        + [pltpu.VMEM(tokens.shape, BF16), pltpu.VMEM((width, ff), BF16)]
         + [slabs] * 6
         + [pltpu.VMEM((chips, 2, rows, ff), BF16)] * 4
         + [pltpu.VMEM((chips, 2, rows, ff), F32), pltpu.VMEM((replicas, rows, ff), BF16)]
-        + [dma((7,)), dma((2,))]
+        + [dma((7,))]
         + [dma((peers,))] * 6
         + [dma((chips, 2))] * 4
         + [dma((chips,))] * 4,

time: 43.1 us -> 40.4 us (0.937)
  local copies, waits for them, and re-layouts: 3.63 us -> 1.54 us
  Pallas kernels: 38.6 us -> 38.1 us
    unnamed x2, local copies, waits for them, and re-layouts: 3.63 us -> 1.54 us
    pallas_call x1, Pallas kernels: 38.6 us -> 38.1 us  [tokens_move(): pl.pallas_call(functools.partial(kernel, experts, replicas), out_shape=(p...]
where the time goes in v5:
time: 40.4 us; the launch traced here: 40.2 us
  Pallas kernels  38.1 us (94%)
  local copies, waits for them, and re-layouts  1.54 us (4%)
  between operations  0.64 us (2%)
    pallas_call x1, Pallas kernels, tokens_move(): pl.pallas_call(functools.partial(kernel, experts, replicas), out_shape=(p...  38.1 us
    unnamed x2, local copies, waits for them, and re-layouts  1.54 us

profile of v5, /device:TPU:0, one launch (start us, length us, event | category | flops | bytes accessed | tf_op | source)
XLA Modules:
  0.0 40.2 jit_solution(8981518407876240212)
XLA Ops:
  0.6 38.1 %shard_map.86 = (bf16[32,2048]{1,0:T(8,128)(2,1)S(1)}, bf16[512,768]{1,0:T(8,128)(2,1)S(1)}) custom-call(bf16[32,2048]{1,0:T(8,128)(2,1)} %tokens_hbm.1, bf16[32,2048]{1,0:T(8,128)(2,1)} %out_grad_hbm.1, s32[2,32]{1,0:T(2,128)} %bitcast.10, f32[2,32]{1,0:T(2,128)} %bitcast.11, bf16[512,768]{1,0:T(8,128)(2,1)} %bitcast.7, bf16[512,768]{1,0:T(8,128)(2,1)} %bitcast.8, ...), custom_call_target="tpu_custom_call" | custom-call | tf_op jit(solution)/shard_map/pallas_call | solution.py:374
  38.7 0.7 %copy.11 = bf16[32,2048]{1,0:T(8,128)(2,1)} copy(bf16[32,2048]{1,0:T(8,128)(2,1)S(1)} %get-tuple-element.6) | data formatting | bytes 262144
  39.4 0.9 %copy.12 = bf16[1,512,768]{2,1,0:T(8,128)(2,1)} copy(bf16[1,512,768]{2,1,0:T(8,128)(2,1)S(1)} %bitcast.6) | data formatting | bytes 1572864

commit v6 on v5

--- a/solution.py
+++ b/solution.py
@@ -36,6 +36,7 @@
     out_grad,
     expert_ids,
     combine,
+    down_t,
     tok_send,
     tok_recv,
     grad_send,
@@ -180,8 +181,9 @@
     fill(grad_send, slot_weight * dot(either, out_grad[...]))
     picks = [pick.astype(BF16) for pick in picks]
     grad_recv[pl.ds(me, 1)] = grad_send[pl.ds(me, 1)]
-    for load in loads[4:6]:
+    for load in loads[4:]:
         load.wait()
+    down_t[...] = down_w[...].T
     grad_copies = exchange(grad_send, grad_recv, grad_ssem, grad_rsem)
 
     def mate_copy(c, i):
@@ -269,12 +271,11 @@
     mate_out = hid_copy(0, r, r, mate_r, fwd_ssem, fwd_rsem)
     mate_in = hid_copy(0, r, mate_r, mate_r, fwd_ssem, fwd_rsem)
     mate_out.start()
-    loads[6].wait()
 
     ret_copies = exchange(ret_send, ret_recv, ret_ssem, ret_rsem)
 
     def give_back(pr):
-        out = dot(hid[pr], down_w[...], ((1,), (1,)))
+        out = dot(hid[pr], down_t[...])
         for pe in range(experts):
             ret_send[pr * experts + pe] = slab(out[pe * CAP : (pe + 1) * CAP])
 
@@ -383,6 +384,7 @@
         + [pltpu.VMEM(tokens.shape, BF16)] * 2
         + [pltpu.VMEM((top, tokens.shape[0]), jnp.int32)]
         + [pltpu.VMEM((top, tokens.shape[0]), F32)]
+        + [pltpu.VMEM((ff, width), BF16)]
         + [slabs] * 6
         + [pltpu.VMEM((chips, 2, rows, ff), BF16)] * 4
         + [pltpu.VMEM((chips, 2, rows, ff), F32), pltpu.VMEM((replicas, rows, ff), BF16)]

time: 40.4 us -> 40.3 us (level)
  no operation moved by 1% of the time
where the time goes in v6:
time: 40.3 us; the launch traced here: 40.1 us
  Pallas kernels  38 us (94%)
  local copies, waits for them, and re-layouts  1.54 us (4%)
  between operations  0.64 us (2%)
    pallas_call x1, Pallas kernels, tokens_move(): pl.pallas_call(functools.partial(kernel, experts, replicas), out_shape=(p...  38 us
    unnamed x2, local copies, waits for them, and re-layouts  1.54 us

profile of v6, /device:TPU:0, one launch (start us, length us, event | category | flops | bytes accessed | tf_op | source)
XLA Modules:
  0.0 40.1 jit_solution(3625801885106782745)
XLA Ops:
  0.6 38.0 %shard_map.86 = (bf16[32,2048]{1,0:T(8,128)(2,1)S(1)}, bf16[512,768]{1,0:T(8,128)(2,1)S(1)}) custom-call(bf16[32,2048]{1,0:T(8,128)(2,1)} %tokens_hbm.1, bf16[32,2048]{1,0:T(8,128)(2,1)} %out_grad_hbm.1, s32[2,32]{1,0:T(2,128)} %bitcast.10, f32[2,32]{1,0:T(2,128)} %bitcast.11, bf16[512,768]{1,0:T(8,128)(2,1)} %bitcast.7, bf16[512,768]{1,0:T(8,128)(2,1)} %bitcast.8, ...), custom_call_target="tpu_custom_call" | custom-call | tf_op jit(solution)/shard_map/pallas_call | solution.py:375
  38.6 0.7 %copy.11 = bf16[32,2048]{1,0:T(8,128)(2,1)} copy(bf16[32,2048]{1,0:T(8,128)(2,1)S(1)} %get-tuple-element.6) | data formatting | bytes 262144
  39.3 0.9 %copy.12 = bf16[1,512,768]{2,1,0:T(8,128)(2,1)} copy(bf16[1,512,768]{2,1,0:T(8,128)(2,1)S(1)} %bitcast.6) | data formatting | bytes 1572864
